TPU v7x, 32 devices: a whole 2x2x4 slice. The times are simulated.
32 devices in a mesh: groups: 2 (over y), ctx: 4 (over z), head: 2 (over x), mem: 2 (over core).
Axes of the slice: x: 2, y: 2, z: 4, core: 2. Of those that a mesh axis runs over, the one named last changes fastest.
Arguments:
- queries: bfloat16 [8192, 2048], P(('groups', 'ctx', 'mem'), 'head'), parts along dimension 0, may hold values from -48 to 48
- keys: bfloat16 [8192, 2048], P(('groups', 'ctx', 'mem'), 'head'), parts along dimension 0, may hold values from -6 to 6
- values: bfloat16 [8192, 2048], P(('groups', 'ctx', 'mem'), 'head'), parts along dimension 0, may hold values from -6 to 6
- memory_keys: bfloat16 [32768, 2048], P(('groups', 'ctx', 'mem'), 'head'), parts along dimension 0, may hold values from -6 to 6
- memory_values: bfloat16 [32768, 2048], P(('groups', 'ctx', 'mem'), 'head'), parts along dimension 0, may hold values from -6 to 6
- retrieval: int32 [128, 8], P(('groups', 'ctx', 'mem')), parts along dimension 0, may hold values from 0 to 255, as said below
- memory_gate: float32 [16], P('head'), may hold values from -1 to 2
Outputs:
- attended: bfloat16 [8192, 2048], P(('groups', 'ctx', 'mem'), 'head'), parts along dimension 0
There are 2 independent parts, one for each index of `groups`. A program takes and returns all parts, laid end to end along the dimension named above; an argument that names none is the same for every part. Nothing has to cross between parts.
Inputs may be any that keep to these rules, and one draw needn't show every extreme that they name: `retrieval`: all ids named by the rows of one device (the 8 ids of each of its query blocks) are distinct. A holder is a block of 32 consecutive memory blocks; from the rows of one device at most 12 ids fall in one holder, and in every device some holder gets exactly 12 of them.
All inputs are finite; a program needn't handle non-finite values.
Results may differ from a plain program's by a relative error of at most 0.0049.
Values may be sent and summed in bfloat16 or wider, within the bound.
A program may use at most 256 MiB of HBM per device.

v0:
```python
import math

import jax
import jax.numpy as jnp
from jax import lax
from jax.sharding import PartitionSpec as P

QBLK = 64
SPAN = 4


def from_behind(x, axis, by):
    length = lax.axis_size(axis)
    pairs = [(i, i + by) for i in range(length) if 0 <= i + by < length]
    return lax.ppermute(x, axis, pairs)


def request_table(retrieval, blocks_held, holders, capacity):
    wanted = retrieval.reshape(-1)
    holder_of = wanted // blocks_held
    local_block = wanted - holder_of * blocks_held
    request_count = wanted.shape[0]
    request_order = jnp.arange(request_count, dtype=jnp.int32)
    same_holder = holder_of[:, None] == holder_of[None, :]
    before = request_order[None, :] < request_order[:, None]
    position_rank = jnp.sum((same_holder & before).astype(jnp.int32), axis=1)
    holder_ids = jnp.arange(holders, dtype=jnp.int32)
    slot_ids = jnp.arange(capacity, dtype=jnp.int32)
    slot_match = (holder_of[:, None, None] == holder_ids[None, :, None]) & (
        position_rank[:, None, None] == slot_ids[None, None, :]
    )
    asked_table = jnp.sum(jnp.where(slot_match, local_block[:, None, None] + 1, 0), axis=0) - 1
    return (asked_table, holder_of * capacity + position_rank)


def body(queries, keys, values, memory_keys, memory_values, retrieval, memory_gate):
    tok_rows, width = queries.shape
    heads_here = memory_gate.shape[0]
    head_size = width // heads_here
    query_blocks, topk = retrieval.shape
    holders = lax.axis_size(("ctx", "mem"))
    place = lax.axis_index(("ctx", "mem"))
    blocks_held = memory_keys.shape[0] // QBLK
    capacity = max(3, 3 * query_blocks * topk // (2 * holders))
    asked_table, slot_index = request_table(retrieval, blocks_held, holders, capacity)
    stored_keys = memory_keys.reshape(blocks_held, QBLK, width)
    stored_values = memory_values.reshape(blocks_held, QBLK, width)
    asked_blocks = lax.all_to_all(
        asked_table, ("ctx", "mem"), split_axis=0, concat_axis=0, tiled=True
    )
    asked_blocks = jnp.maximum(asked_blocks, 0)
    fetched_keys, fetched_values = (
        lax.all_to_all(
            stored_keys[asked_blocks], ("ctx", "mem"), split_axis=0, concat_axis=0, tiled=True
        ),
        lax.all_to_all(
            stored_values[asked_blocks], ("ctx", "mem"), split_axis=0, concat_axis=0, tiled=True
        ),
    )
    got_keys = fetched_keys.reshape(holders * capacity, QBLK, width)[slot_index].reshape(
        query_blocks, topk * QBLK, width
    )
    got_values = fetched_values.reshape(holders * capacity, QBLK, width)[slot_index].reshape(
        query_blocks, topk * QBLK, width
    )
    stacked = jnp.stack([keys, values])
    earlier = [from_behind(stacked, ("ctx", "mem"), distance) for distance in range(1, SPAN + 1)]
    window = jnp.concatenate(earlier[::-1] + [stacked], axis=1)
    window_keys = window[0]
    window_values = window[1]
    score_scale = 1.0 / math.sqrt(head_size)
    query_pos = place * tok_rows + jnp.arange(tok_rows, dtype=jnp.int32)
    key_pos = (place - SPAN) * tok_rows + jnp.arange((SPAN + 1) * tok_rows, dtype=jnp.int32)
    in_window = (
        (key_pos[None, :] <= query_pos[:, None])
        & (key_pos[None, :] > query_pos[:, None] - SPAN * tok_rows)
        & (key_pos[None, :] >= 0)
    )
    per_head = []
    for head_index in range(heads_here):
        col_start = head_index * head_size
        col_end = col_start + head_size
        query_head = queries[:, col_start:col_end]
        near_scores = (
            jnp.einsum(
                "qd,kd->qk",
                query_head,
                window_keys[:, col_start:col_end],
                preferred_element_type=jnp.float32,
            )
            * score_scale
        )
        near_scores = jnp.where(in_window, near_scores, -1e30)
        far_scores = (
            jnp.einsum(
                "nhs,nos->nho",
                query_head.reshape(query_blocks, QBLK, head_size),
                got_keys[:, :, col_start:col_end],
                preferred_element_type=jnp.float32,
            )
            * score_scale
            + memory_gate[head_index]
        )
        far_scores = far_scores.reshape(tok_rows, topk * QBLK)
        row_max = jnp.maximum(jnp.max(near_scores, axis=1), jnp.max(far_scores, axis=1))
        near_exp = jnp.exp(near_scores - row_max[:, None])
        far_exp = jnp.exp(far_scores - row_max[:, None])
        denominator = jnp.sum(near_exp, axis=1) + jnp.sum(far_exp, axis=1)
        near_weights = (near_exp / denominator[:, None]).astype(jnp.bfloat16)
        far_weights = (far_exp / denominator[:, None]).astype(jnp.bfloat16)
        near_part = jnp.dot(
            near_weights, window_values[:, col_start:col_end], preferred_element_type=jnp.float32
        )
        far_part = jnp.einsum(
            "fkm,fmp->fkp",
            far_weights.reshape(query_blocks, QBLK, topk * QBLK),
            got_values[:, :, col_start:col_end],
            preferred_element_type=jnp.float32,
        )
        per_head.append(near_part + far_part.reshape(tok_rows, head_size))
    return jnp.concatenate(per_head, axis=1).astype(jnp.bfloat16)


def solution(mesh):
    placed = (
        P(("groups", "ctx", "mem"), "head"),
        P(("groups", "ctx", "mem"), "head"),
        P(("groups", "ctx", "mem"), "head"),
        P(("groups", "ctx", "mem"), "head"),
        P(("groups", "ctx", "mem"), "head"),
        P(("groups", "ctx", "mem"), None),
        P("head"),
    )
    return jax.shard_map(
        body,
        mesh=mesh,
        in_specs=placed,
        out_specs=P(("groups", "ctx", "mem"), "head"),
        check_vma=False,
    )
```

profile of v0, /device:TPU:16, one launch (start us, length us, event | category | flops | bytes accessed | tf_op | source)
XLA Modules:
  0.0 968.1 jit_solution(4126333561716352185)
XLA Ops:
  1.4 8.2 all_to_all.16
  9.7 9.1 gather_fusion.2
  18.7 7.6 all-to-all-start.2
  26.3 9.0 gather_fusion
  35.3 261.5 %all-to-all-done.2 = bf16[8,12,64,1024]{3,2,1,0:T(8,128)(2,1)} async-done(((bf16[8,12,64,1024]{3,2,1,0:T(8,128)(2,1)}), bf16[8,12,64,1024]{3,2,1,0:T(8,128)(2,1)}, u32[]{:S(2)}, u32[]{:S(2)}) %all-to-all-start.2) | async-done | bytes 12582944 | tf_op jit(solution)/shard_map/all_to_all | solution.py:56
  296.9 9.0 all-to-all-start.1
  305.8 1.5 pad_maximum_fusion
  307.3 1.3 collective-permute-start
  308.6 3.1 collective-permute-start.1
  311.8 1.9 collective-permute-start.2
  313.7 1.9 collective-permute-start.3
  318.5 236.5 %collective-permute-done = bf16[2,512,1024]{2,1,0:T(8,128)(2,1)} collective-permute-done((bf16[2,512,1024]{2,1,0:T(8,128)(2,1)}, bf16[2,512,1024]{2,1,0:T(8,128)(2,1)}, u32[]{:S(2)}, u32[]{:S(2)}) %collective-permute-start) | collective-permute-done | bytes 2097184 | tf_op jit(solution)/shard_map/ppermute | solution.py:15
  555.0 3.1 constant_dynamic-update-slice_fusion.4
  558.1 41.3 %collective-permute-done.1 = bf16[2,512,1024]{2,1,0:T(8,128)(2,1)} collective-permute-done((bf16[2,512,1024]{2,1,0:T(8,128)(2,1)}, bf16[2,512,1024]{2,1,0:T(8,128)(2,1)}, u32[]{:S(2)}, u32[]{:S(2)}) %collective-permute-start.1) | collective-permute-done | bytes 2097184 | tf_op jit(solution)/shard_map/ppermute | solution.py:15
  599.4 3.1 constant_dynamic-update-slice_fusion.3
  602.5 176.9 %collective-permute-done.2 = bf16[2,512,1024]{2,1,0:T(8,128)(2,1)} collective-permute-done((bf16[2,512,1024]{2,1,0:T(8,128)(2,1)}, bf16[2,512,1024]{2,1,0:T(8,128)(2,1)}, u32[]{:S(2)}, u32[]{:S(2)}) %collective-permute-start.2) | collective-permute-done | bytes 2097184 | tf_op jit(solution)/shard_map/ppermute | solution.py:15
  779.4 3.1 constant_dynamic-update-slice_fusion.2
  782.5 19.3 %collective-permute-done.3 = bf16[2,512,1024]{2,1,0:T(8,128)(2,1)} collective-permute-done((bf16[2,512,1024]{2,1,0:T(8,128)(2,1)}, bf16[2,512,1024]{2,1,0:T(8,128)(2,1)}, u32[]{:S(2)}, u32[]{:S(2)}) %collective-permute-start.3) | collective-permute-done | bytes 2097184 | tf_op jit(solution)/shard_map/ppermute | solution.py:15
  801.8 3.1 constant_dynamic-update-slice_fusion.1
  804.9 1.5 constant_dynamic-update-slice_fusion
  806.5 9.2 slice_bitcast_fusion
  815.7 4.7 fusion.132
  820.5 4.6 fusion.134
  825.1 4.5 fusion.136
  829.7 4.5 fusion.138
  834.3 4.6 fusion.140
  839.0 4.5 fusion.142
  843.6 4.6 fusion.144
  848.3 4.6 fusion.146
  852.9 10.2 %gather_fusion.3 = bf16[64,64,1024]{2,1,0:T(8,128)(2,1)} fusion(bf16[96,64,1024]{2,1,0:T(8,128)(2,1)} %bitcast.18, s32[1024]{0:T(1024)S(1)} %pad_clamp_fusion), kind=kCustom, calls=%fused_computation.3 | custom fusion | bytes 16777472 | tf_op jit(solution)/shard_map/gather | solution.py:63
  863.2 10.4 %gather_fusion.1 = bf16[64,64,1024]{2,1,0:T(8,128)(2,1)} fusion(bf16[96,64,1024]{2,1,0:T(8,128)(2,1)} %bitcast.8, s32[1024]{0:T(1024)S(1)} %pad_clamp_fusion), kind=kCustom, calls=%fused_computation.1 | custom fusion | bytes 16777472 | tf_op jit(solution)/shard_map/gather | solution.py:60
  873.6 2.4 fusion.133
  876.0 3.3 fusion
  879.9 1.6 fusion.77
  882.2 2.5 fusion.135
  884.8 3.3 fusion.1
  888.6 1.6 fusion.74
  890.9 2.4 fusion.137
  893.4 3.3 fusion.2
  897.2 1.6 fusion.71
  899.6 2.4 fusion.139
  902.1 3.3 fusion.3
  905.9 1.6 fusion.68
  908.2 2.4 fusion.141
  910.7 3.3 fusion.4
  914.5 1.6 fusion.65
  916.8 2.5 fusion.143
  919.4 3.3 fusion.5
  923.2 1.6 fusion.62
  926.3 2.3 fusion.145
  929.3 3.5 fusion.6
  933.3 1.6 fusion.59
  936.4 2.5 fusion.147
  939.7 3.3 fusion.7
  943.4 2.4 fusion.56
  945.9 1.8 copy.56
  947.7 3.8 fusion.55
  951.6 3.7 fusion.54
  955.4 3.7 fusion.53
  959.2 1.1 fusion.52
  960.5 1.1 fusion.51
  963.7 1.1 fusion.49
  965.3 1.1 fusion.48
  966.3 1.3 copy.57
  (194 shorter events, 20.4 us)
Async XLA Ops:
  18.7 278.1 %all-to-all-start.2 = ((bf16[8,12,64,1024]{3,2,1,0:T(8,128)(2,1)}), bf16[8,12,64,1024]{3,2,1,0:T(8,128)(2,1)}, u32[]{:S(2)}, u32[]{:S(2)}) async-start(bf16[8,12,64,1024]{3,2,1,0:T(8,128)(2,1)} %bitcast.88), calls=%async_computation.2 | async-start | bytes 25165824 | tf_op jit(solution)/shard_map/all_to_all | solution.py:56
  296.8 9.0 copy-start
  296.8 9.0 copy-start.1
  296.8 18.8 %copy-start.12 = (s32[8,8]{1,0:T(8,128)S(1)}, s32[8,8]{1,0:T(8,128)}, u32[]{:S(2)}) copy-start(s32[8,8]{1,0:T(8,128)} %param.12) | copy-start | bytes 772
  296.8 20.1 %copy-start.11 = (f32[8]{0:T(128)S(1)}, f32[8]{0:T(128)}, u32[]{:S(2)}) copy-start(f32[8]{0:T(128)} %param.13) | copy-start | bytes 100
  296.8 20.8 %copy-start.2 = (bf16[512,1024]{1,0:T(8,128)(2,1)S(1)}, bf16[512,1024]{1,0:T(8,128)(2,1)}, u32[]{:S(2)}) copy-start(bf16[512,1024]{1,0:T(8,128)(2,1)} %param.7) | copy-start | bytes 3145732
  296.9 566.3 %all-to-all-start.1 = ((bf16[8,12,64,1024]{3,2,1,0:T(8,128)(2,1)}), bf16[8,12,64,1024]{3,2,1,0:T(8,128)(2,1)}, u32[]{:S(2)}, u32[]{:S(2)}) async-start(bf16[8,12,64,1024]{3,2,1,0:T(8,128)(2,1)} %bitcast.87), calls=%async_computation.1 | async-start | bytes 25165824 | tf_op jit(solution)/shard_map/all_to_all | solution.py:53
  307.3 247.7 %collective-permute-start = (bf16[2,512,1024]{2,1,0:T(8,128)(2,1)}, bf16[2,512,1024]{2,1,0:T(8,128)(2,1)}, u32[]{:S(2)}, u32[]{:S(2)}) collective-permute-start(bf16[2,512,1024]{2,1,0:T(8,128)(2,1)} %pad_maximum_fusion), channel_id=1, source_target_pairs={{0,8},{1,9},{4,12},{5,13},{2,10},{3,11},{6,14},{7,15},{16,24},{17,... | collective-permute-start | bytes 6291464 | tf_op jit(solution)/shard_map/ppermute | solution.py:15
  308.6 290.8 %collective-permute-start.1 = (bf16[2,512,1024]{2,1,0:T(8,128)(2,1)}, bf16[2,512,1024]{2,1,0:T(8,128)(2,1)}, u32[]{:S(2)}, u32[]{:S(2)}) collective-permute-start(bf16[2,512,1024]{2,1,0:T(8,128)(2,1)} %pad_maximum_fusion), channel_id=1, source_target_pairs={{0,5},{1,8},{4,9},{5,12},{8,13},{2,7},{3,10},{6,11},{7,14},{10,15}... | collective-permute-start | bytes 6291464 | tf_op jit(solution)/shard_map/ppermute | solution.py:15
  311.8 467.6 %collective-permute-start.2 = (bf16[2,512,1024]{2,1,0:T(8,128)(2,1)}, bf16[2,512,1024]{2,1,0:T(8,128)(2,1)}, u32[]{:S(2)}, u32[]{:S(2)}) collective-permute-start(bf16[2,512,1024]{2,1,0:T(8,128)(2,1)} %pad_maximum_fusion), channel_id=1, source_target_pairs={{0,4},{1,5},{4,8},{5,9},{8,12},{9,13},{2,6},{3,7},{6,10},{7,11},{1... | collective-permute-start | bytes 6291464 | tf_op jit(solution)/shard_map/ppermute | solution.py:15
  313.7 488.1 %collective-permute-start.3 = (bf16[2,512,1024]{2,1,0:T(8,128)(2,1)}, bf16[2,512,1024]{2,1,0:T(8,128)(2,1)}, u32[]{:S(2)}, u32[]{:S(2)}) collective-permute-start(bf16[2,512,1024]{2,1,0:T(8,128)(2,1)} %pad_maximum_fusion), channel_id=1, source_target_pairs={{0,1},{1,4},{4,5},{5,8},{8,9},{9,12},{12,13},{2,3},{3,6},{6,7},{7,... | collective-permute-start | bytes 6291464 | tf_op jit(solution)/shard_map/ppermute | solution.py:15
  806.5 9.2 copy-start.22
  806.5 9.2 copy-start.30
  806.5 9.2 copy-start.31
  852.8 10.3 %copy-start.21 = (f32[512]{0:T(512)}, f32[512]{0:T(512)S(1)}, u32[]{:S(2)}) copy-start(f32[512]{0:T(512)S(1)} %get-tuple-element.53) | copy-start | bytes 6148
  863.1 10.4 %copy-start.10 = (bf16[512,128]{1,0:T(8,128)(2,1)S(1)}, bf16[512,128]{1,0:T(8,128)(2,1)}, u32[]{:S(2)}) copy-start(bf16[512,128]{1,0:T(8,128)(2,1)} %get-tuple-element.15) | copy-start | bytes 393220
  876.0 6.2 copy-start.9
  884.8 6.2 copy-start.8
  902.1 3.3 copy-start.13
  910.7 3.4 copy-start.15
  910.7 6.1 copy-start.7
  919.4 3.3 copy-start.17
  919.4 6.9 copy-start.6
  928.7 0.6 copy-start.19
  939.7 8.0 copy-start.23
  943.4 8.1 slice-start
  947.7 4.0 slice-start.1
  947.7 3.9 copy-start.24
  951.6 3.7 copy-start.25
  951.6 7.4 slice-start.10
  955.3 3.7 slice-start.11
  955.4 3.7 copy-start.14
  955.4 3.7 copy-start.26
  955.4 4.9 slice-start.8
  959.1 1.3 slice-start.9
  959.1 1.3 copy-start.16
  959.2 1.3 copy-start.27
  959.2 2.6 slice-start.6
  960.4 1.6 slice-start.7
  960.4 1.7 copy-start.3
  960.5 1.7 copy-start.18
  960.5 1.6 copy-start.28
  960.5 3.0 slice-start.4
  962.1 1.5 slice-start.5
  962.1 1.6 copy-start.4
  962.1 1.5 copy-start.20
  962.1 1.5 copy-start.29
  962.1 2.9 slice-start.2
  963.7 1.6 slice-start.3
  963.7 1.6 copy-start.5
where the time goes:
time: 975 us; the launch traced here: 968 us
  waiting for transfers between devices  736 us (75%)
  matrix products  86.2 us (9%)
  local copies, waits for them, and re-layouts  73.4 us (8%)
  other arithmetic  38.9 us (4%)
  starting transfers between devices  24.8 us (3%)
    ppermute x4, waiting for transfers between devices, from_behind(): return lax.ppermute(x, axis, pairs)  474 us
    all_to_all x1, waiting for transfers between devices, body(): lax.all_to_all(stored_values[asked_blocks], ('ctx', 'mem'), split_axis=0,...  262 us
    dot_general x8, matrix products, body(): jnp.einsum('qd,kd->qk', query_head, window_keys[:, col_start:col_end], pr...  36.6 us
    reduce_sum x16, other arithmetic, body(): denominator = jnp.sum(near_exp, axis=1) + jnp.sum(far_exp, axis=1)  29.3 us
  transfers between devices with their start and end apart: 6, of which 5 were waited for; matrix products, arithmetic and copies ran while one was open for 9% of the time, Pallas kernels for 0%

commit v1 on v0

v1 whole, which is shorter than its diff:
```python
import functools
import math

import jax
import jax.numpy as jnp
from jax import lax
from jax.experimental import pallas as pl
from jax.experimental.pallas import tpu as pltpu
from jax.sharding import PartitionSpec as P

QBLK = 64
SPAN = 4
LOW = -1e30
MESH = pl.DeviceIdType.MESH
NT = (((1,), (1,)), ((), ()))


def slot_tables(everyone, place, blocks_held, sources, capacity):
    ids = everyone.reshape(sources, -1)
    topk = everyone.shape[1]
    mine = (ids // blocks_held) == place
    rank = jnp.cumsum(mine.astype(jnp.int32), axis=1) - 1
    slots = jnp.arange(capacity, dtype=jnp.int32)
    match = mine[:, :, None] & (rank[:, :, None] == slots[None, None, :])
    entry = jnp.arange(ids.shape[1], dtype=jnp.int32)[None, :, None]
    packed = (entry // topk) * blocks_held + (ids % blocks_held)[:, :, None]
    table = jnp.sum(jnp.where(match, packed, 0), axis=1)
    count = jnp.sum(mine.astype(jnp.int32), axis=1)
    return jnp.concatenate([table, count[:, None]], axis=1)


def local_kernel(
    heads, blocks_held, capacity, place_ref, table_ref, gate_ref,
    q_ref, k_ref, v_ref, mk_ref, mv_ref, o_ref, lse_ref, acc, mref, lref,
):
    src = pl.program_id(0)
    rows = q_ref.shape[1]
    size = q_ref.shape[2] // heads
    scale = 1.0 / math.sqrt(size)
    dist = src - place_ref[0]

    def cols_of(h):
        return pl.ds(pl.multiple_of(h * size, size), size)

    def near(kind):
        tile = rows // 2

        @pl.loop(0, heads)
        def _(h):
            cols = cols_of(h)
            k = k_ref[:, cols]
            v = jnp.concatenate([v_ref[:, cols], jnp.ones((rows, size), jnp.bfloat16)], axis=1)
            for part in range(2):
                at = pl.ds(part * tile, tile)
                s = lax.dot_general(q_ref[0, at, cols], k, NT, preferred_element_type=jnp.float32) * scale
                if kind != 1:
                    qi = part * tile + lax.broadcasted_iota(jnp.int32, (tile, rows), 0)
                    ki = lax.broadcasted_iota(jnp.int32, (tile, rows), 1)
                    s = jnp.where(ki <= qi if kind == 0 else ki > qi, s, LOW)
                top = jnp.max(s, axis=1, keepdims=True)
                p = jnp.exp(s - top)
                if kind == 2:
                    p = jnp.where(ki > qi, p, 0.0)
                both = jnp.dot(p.astype(jnp.bfloat16), v, preferred_element_type=jnp.float32)
                acc[at, cols] = both[:, :size]
                lref[at, cols] = both[:, size:]
                mref[at, cols] = jnp.broadcast_to(top, (tile, size))

    @pl.when(dist == 0)
    def _():
        near(0)

    @pl.when((dist > 0) & (dist < SPAN))
    def _():
        near(1)

    @pl.when(dist == SPAN)
    def _():
        near(2)

    @pl.when((dist < 0) | (dist > SPAN))
    def _():
        acc[...] = jnp.zeros_like(acc)
        lref[...] = jnp.zeros_like(lref)
        mref[...] = jnp.full_like(mref, LOW)

    def slot(i, carry):
        packed = table_ref[src, i]
        at = pl.ds(pl.multiple_of((packed // blocks_held) * QBLK, QBLK), QBLK)
        mat = pl.ds(pl.multiple_of((packed % blocks_held) * QBLK, QBLK), QBLK)
        for h in range(heads):
            cols = slice(h * size, (h + 1) * size)
            s = lax.dot_general(q_ref[0, at, cols], mk_ref[mat, cols], NT, preferred_element_type=jnp.float32)
            s = s * scale + gate_ref[h]
            old = mref[at, cols]
            new = jnp.maximum(old, jnp.max(s, axis=1, keepdims=True))
            keep = jnp.exp(old - new)
            p = jnp.exp(s - new[:, :QBLK])
            pv = jnp.dot(p.astype(jnp.bfloat16), mv_ref[mat, cols], preferred_element_type=jnp.float32)
            acc[at, cols] = acc[at, cols] * keep + pv
            lref[at, cols] = lref[at, cols] * keep + jnp.sum(p, axis=1, keepdims=True)
            mref[at, cols] = new
        return carry

    lax.fori_loop(0, table_ref[src, capacity], slot, 0)

    step = 128

    @pl.loop(0, rows // step)
    def _(r):
        at = pl.ds(pl.multiple_of(r * step, step), step)
        lane = lax.broadcasted_iota(jnp.int32, (step, 128), 1)
        stats = jnp.full((step, 128), LOW, jnp.float32)
        for h in range(heads):
            cols = slice(h * size, (h + 1) * size)
            l = lref[at, cols]
            some = l > 0.0
            safe = jnp.where(some, l, 1.0)
            o_ref[0, at, cols] = (acc[at, cols] / safe).astype(jnp.bfloat16)
            lse = jnp.where(some, mref[at, cols] + jnp.log(safe), LOW)
            stats = jnp.where(lane == h, lse, stats)
        lse_ref[0, :, at] = stats.T[: lse_ref.shape[1]]


def partials(q_all, keys, values, mkeys, mvalues, gate, place, table, capacity):
    sources, rows, width = q_all.shape
    heads = gate.shape[0]
    stat_rows = -(-heads // 8) * 8
    whole = lambda a: pl.BlockSpec(a.shape, lambda s: (0,) * a.ndim)
    smem = pl.BlockSpec(memory_space=pltpu.SMEM)
    per = pl.BlockSpec((1, rows, width), lambda s: (s, 0, 0))
    return pl.pallas_call(
        functools.partial(local_kernel, heads, mkeys.shape[0] // QBLK, capacity),
        grid=(sources,),
        in_specs=[smem, smem, smem, per, whole(keys), whole(values), whole(mkeys), whole(mvalues)],
        out_specs=[per, pl.BlockSpec((1, stat_rows, rows), lambda s: (s, 0, 0))],
        out_shape=[
            jax.ShapeDtypeStruct(q_all.shape, jnp.bfloat16),
            jax.ShapeDtypeStruct((sources, stat_rows, rows), jnp.float32),
        ],
        scratch_shapes=[pltpu.VMEM((rows, width), jnp.float32)] * 3,
        compiler_params=pltpu.CompilerParams(vmem_limit_bytes=56 * 2**20),
    )(place, table, gate, q_all, keys, values, mkeys, mvalues)


def merge_kernel(
    heads, chips, o_hbm, lse_hbm, out_ref,
    own, own_s, twin, twin_s, left, left_s, right, right_s,
    load_sem, load_s_sem, tsend, tsend_s, trecv, trecv_s,
    usend, usend_s, urecv, urecv_s, dsend, dsend_s, drecv, drecv_s,
):
    c = lax.axis_index("ctx")
    m = lax.axis_index("mem")
    rows, width = out_ref.shape
    size = width // heads
    last = chips - 1

    barrier = pltpu.get_barrier_semaphore()
    pl.semaphore_signal(barrier, inc=1, device_id={"mem": 1 - m}, device_id_type=MESH)

    @pl.when(c > 0)
    def _():
        pl.semaphore_signal(barrier, inc=1, device_id={"ctx": c - 1}, device_id_type=MESH)

    @pl.when(c < last)
    def _():
        pl.semaphore_signal(barrier, inc=1, device_id={"ctx": c + 1}, device_id_type=MESH)

    inner = (c > 0).astype(jnp.int32) + (c < last).astype(jnp.int32)
    pl.semaphore_wait(barrier, 1 + inner)

    def remote(src, dst, ss, rs, where):
        return pltpu.make_async_remote_copy(
            src_ref=src, dst_ref=dst, send_sem=ss, recv_sem=rs, device_id=where, device_id_type=MESH
        )

    def loads(d):
        return (
            pltpu.make_async_copy(o_hbm.at[2 * d + m], own.at[d], load_sem.at[d]),
            pltpu.make_async_copy(lse_hbm.at[2 * d + m], own_s.at[d], load_s_sem.at[d]),
        )

    def twins(d):
        other = {"mem": 1 - m}
        return (
            remote(o_hbm.at[2 * d + 1 - m], twin.at[d], tsend.at[d], trecv.at[d], other),
            remote(lse_hbm.at[2 * d + 1 - m], twin_s.at[d], tsend_s.at[d], trecv_s.at[d], other),
        )

    def ups(d):
        where = {"ctx": c + 1}
        return (
            remote(own.at[d], left.at[d], usend.at[d], urecv.at[d], where),
            remote(own_s.at[d], left_s.at[d], usend_s.at[d], urecv_s.at[d], where),
        )

    def downs(d):
        where = {"ctx": c - 1}
        return (
            remote(own.at[d], right.at[d], dsend.at[d], drecv.at[d], where),
            remote(own_s.at[d], right_s.at[d], dsend_s.at[d], drecv_s.at[d], where),
        )

    order = []
    for i in range(chips):
        for d in (last - i, i):
            if d not in order:
                order.append(d)
    for d in order:
        for copy in twins(d) + loads(d):
            copy.start()

    def combine(d, into, others):
        parts = [own] + [o for o, _ in others]
        stats = [own_s[d]] + [s[d] for _, s in others]
        top = functools.reduce(jnp.maximum, stats)
        weights = [jnp.exp(s - top) for s in stats]
        total = functools.reduce(jnp.add, weights)
        own_s[d] = top + jnp.log(total)
        shares = [(w / total).T for w in weights]
        step = 64
        for r in range(rows // step):
            at = slice(r * step, (r + 1) * step)
            for h in range(heads):
                cols = slice(h * size, (h + 1) * size)
                out = None
                for part, share in zip(parts, shares):
                    term = part[d, at, cols].astype(jnp.float32) * share[at, h : h + 1]
                    out = term if out is None else out + term
                into(at, cols, out.astype(jnp.bfloat16))

    def wait_local(d):
        for copy in loads(d):
            copy.wait()
        for copy in twins(d):
            copy.wait()

    def store_own(d):
        def put(at, cols, value):
            own[d, at, cols] = value
        return put

    def store_out(at, cols, value):
        out_ref[at, cols] = value

    def visit_up(d):
        wait_local(d)

        @pl.when(c == 0)
        def _():
            combine(d, store_own(d), [(twin, twin_s)])

        @pl.when(c > 0)
        def _():
            for copy in ups(d):
                copy.wait_recv()
            combine(d, store_own(d), [(twin, twin_s), (left, left_s)])

        for copy in ups(d):
            copy.start()

    def visit_down(d):
        wait_local(d)

        @pl.when(c == last)
        def _():
            combine(d, store_own(d), [(twin, twin_s)])

        @pl.when(c < last)
        def _():
            for copy in downs(d):
                copy.wait_recv()
            combine(d, store_own(d), [(twin, twin_s), (right, right_s)])

        for copy in downs(d):
            copy.start()

    @pl.loop(0, last)
    def _(i):
        @pl.when(last - i > c)
        def _():
            visit_up(last - i)

        @pl.when(i < c)
        def _():
            visit_down(i)

    wait_local(c)

    @pl.when(c == 0)
    def _():
        for copy in downs(c):
            copy.wait_recv()
        combine(c, store_out, [(twin, twin_s), (right, right_s)])

    @pl.when(c == last)
    def _():
        for copy in ups(c):
            copy.wait_recv()
        combine(c, store_out, [(twin, twin_s), (left, left_s)])

    @pl.when((c > 0) & (c < last))
    def _():
        for copy in ups(c) + downs(c):
            copy.wait_recv()
        combine(c, store_out, [(twin, twin_s), (left, left_s), (right, right_s)])

    @pl.loop(0, chips)
    def _(d):
        @pl.when(d > c)
        def _():
            for copy in ups(d):
                copy.wait_send()

        @pl.when(d < c)
        def _():
            for copy in downs(d):
                copy.wait_send()


def merged(o, lse, heads):
    sources, rows, width = o.shape
    chips = sources // 2
    big = pltpu.VMEM((chips, rows, width), jnp.bfloat16)
    small = pltpu.VMEM((chips,) + lse.shape[1:], jnp.float32)
    return pl.pallas_call(
        functools.partial(merge_kernel, heads, chips),
        in_specs=[pl.BlockSpec(memory_space=pl.ANY)] * 2,
        out_specs=pl.BlockSpec(memory_space=pltpu.VMEM),
        out_shape=jax.ShapeDtypeStruct((rows, width), jnp.bfloat16),
        scratch_shapes=[big, small] * 4 + [pltpu.SemaphoreType.DMA((chips,))] * 14,
        compiler_params=pltpu.CompilerParams(
            collective_id=0, has_side_effects=True, vmem_limit_bytes=56 * 2**20
        ),
    )(o, lse)


def body(queries, keys, values, memory_keys, memory_values, retrieval, memory_gate):
    axes = ("ctx", "mem")
    sources = lax.axis_size(axes)
    place = lax.axis_index(axes)
    query_blocks, topk = retrieval.shape
    capacity = max(3, 3 * query_blocks * topk // (2 * sources))
    blocks_held = memory_keys.shape[0] // QBLK
    everyone = lax.all_gather(retrieval, axes, axis=0, tiled=True)
    table = slot_tables(everyone, place, blocks_held, sources, capacity)
    q_all = lax.all_gather(queries, axes, axis=0)
    o, lse = partials(
        q_all, keys, values, memory_keys, memory_values, memory_gate,
        place.reshape(1).astype(jnp.int32), table, capacity,
    )
    return merged(o, lse, memory_gate.shape[0])


def solution(mesh):
    rows = P(("groups", "ctx", "mem"), "head")
    return jax.shard_map(
        body,
        mesh=mesh,
        in_specs=(rows, rows, rows, rows, rows, P(("groups", "ctx", "mem"), None), P("head")),
        out_specs=rows,
        check_vma=False,
    )
```

time: 975 us -> 424 us (0.43)
  the two profiles are of different devices: /device:TPU:16 before, /device:TPU:20 now
where the time goes in v1:
time: 424 us; the launch traced here: 417 us
  Pallas kernels  317 us (75%)
  waiting for transfers between devices  69.9 us (16%)
  between operations  13.4 us (3%)
  blocking collectives  12.3 us (3%)
    pallas_call x1, Pallas kernels, merged(): pl.pallas_call(functools.partial(merge_kernel, heads, chips), in_specs=[p...  161 us
    pallas_call x1, Pallas kernels, partials(): pl.pallas_call(functools.partial(local_kernel, heads, mkeys.shape[0] // Q...  156 us
    all_gather x1, waiting for transfers between devices, body(): q_all = lax.all_gather(queries, axes, axis=0)  69.2 us
    all_gather x1, blocking collectives, body(): everyone = lax.all_gather(retrieval, axes, axis=0, tiled=True)  12.3 us
  transfers between devices with their start and end apart: 1, of which 1 were waited for; matrix products, arithmetic and copies ran while one was open for 0% of the time, Pallas kernels for 0%

profile of v1, /device:TPU:20, one launch (start us, length us, event | category | flops | bytes accessed | tf_op | source)
XLA Modules:
  0.0 416.8 jit_solution(3640758597559158485)
XLA Ops:
  6.5 0.0 all-gather.3.cloned.1.call-start
  6.5 0.7 all-gather.3.cloned.1.call-update
  7.3 12.3 %all_gather.9 = s32[64,8]{1,0:T(8,128)S(1)} all-gather(s32[8,8]{1,0:T(8,128)} %param.12), channel_id=1, replica_groups=mesh['groups'=2,'ctx'=4,'head'=2,'mem'=2] {'ctx','mem'}, dimensions={0}, use_global_device_ids=true | all-gather | bytes 2304 | tf_op jit(solution)/shard_map/all_gather | solution.py:345
  19.6 0.1 reshape.149
  19.7 0.1 convert_reduce_fusion
  19.8 0.1 reduce_sum.27
  19.9 0.1 reduce_sum.28
  20.0 0.1 copy.11
  20.1 0.2 reduce_window_sum.11
  20.4 0.3 select_reduce_fusion
  20.6 0.1 copy.10
  20.7 0.7 pad_add_fusion.table_ref
  21.4 69.2 %all-gather.3.cloned.1.call-done = bf16[4096,1024]{1,0:T(8,128)(2,1)} async-done(((bf16[512,1024]{1,0:T(8,128)(2,1)}), bf16[4096,1024]{1,0:T(8,128)(2,1)}) %all-gather.3.cloned.1.call-update) | async-done | bytes 8388624 | tf_op jit(solution)/shard_map/all_gather | solution.py:347
  90.6 156.1 %shard_map.73 = (bf16[8,512,1024]{2,1,0:T(8,128)(2,1)}, f32[8,8,512]{2,1,0:T(8,128)}) custom-call(s32[1]{0:T(128)} %bitcast.place_ref, s32[8,13]{1,0:T(8,128)} %pad_add_fusion.table_ref, f32[8]{0:T(128)} %gate_ref.1, bf16[8,512,1024]{2,1,0:T(8,128)(2,1)} %bitcast.3, bf16[512,1024]{1,0:T(8,128)(2,1)} %k_ref.1, bf16[512,1024]{1,0:T(8,128)(2,1)} %v_ref.1, ...), custom_call_target="tpu_custom_call" | custom-call | tf_op jit(solution)/shard_map/pallas_call | solution.py:132
  246.7 161.0 %shard_map.74 = bf16[512,1024]{1,0:T(8,128)(2,1)} custom-call(bf16[8,512,1024]{2,1,0:T(8,128)(2,1)} %get-tuple-element.7.o_hbm, f32[8,8,512]{2,1,0:T(8,128)} %get-tuple-element.8.lse_hbm), custom_call_target="tpu_custom_call" | custom-call | tf_op jit(solution)/shard_map/pallas_call | solution.py:326
  407.7 2.3 copy.13
  (3 shorter events, 0.0 us)
Async XLA Ops:
  6.5 84.1 %all-gather.3.cloned.1.call-start = ((), (), s32[]{:S(2)}) async-start(), calls=%async_computation | async-start | bytes 9437184 | tf_op jit(solution)/shard_map/all_gather | solution.py:347
Sparse Core Ops, SparseCore 0:
  9.0 81.6 all-gather.2

commit v2 on v1

v2 whole, which is shorter than its diff:
```python
import functools
import math

import jax
import jax.numpy as jnp
from jax import lax
from jax.experimental import pallas as pl
from jax.experimental.pallas import tpu as pltpu
from jax.sharding import PartitionSpec as P

QBLK = 64
SPAN = 4
LOW = -1e30
LOG2E = math.log2(math.e)
MESH = pl.DeviceIdType.MESH
NT = (((1,), (1,)), ((), ()))


def slot_tables(everyone, place, blocks_held, sources, capacity):
    ids = everyone.reshape(sources, -1)
    topk = everyone.shape[1]
    mine = (ids // blocks_held) == place
    rank = jnp.cumsum(mine.astype(jnp.int32), axis=1) - 1
    slots = jnp.arange(capacity, dtype=jnp.int32)
    match = mine[:, :, None] & (rank[:, :, None] == slots[None, None, :])
    entry = jnp.arange(ids.shape[1], dtype=jnp.int32)[None, :, None]
    packed = (entry // topk) * blocks_held + (ids % blocks_held)[:, :, None]
    table = jnp.sum(jnp.where(match, packed, 0), axis=1)
    count = jnp.sum(mine.astype(jnp.int32), axis=1)
    return jnp.concatenate([table, count[:, None]], axis=1)


def local_kernel(
    heads, blocks_held, capacity, place_ref, table_ref, gate_ref,
    q_ref, k_ref, v_ref, mk_ref, mv_ref, o_ref, lse_ref, acc, mref, lref,
):
    src = pl.program_id(0)
    rows = q_ref.shape[1]
    size = q_ref.shape[2] // heads
    scale = LOG2E / math.sqrt(size)
    dist = src - place_ref[0]

    def near(kind):
        tile = rows // 2

        @pl.loop(0, heads, unroll=2)
        def _(h):
            cols = pl.ds(pl.multiple_of(h * size, size), size)
            for part in range(2):
                first, count = 0, rows
                if kind == 0 and part == 0:
                    count = tile
                if kind == 2 and part == 1:
                    first, count = tile, tile
                at = pl.ds(part * tile, tile)
                seen = pl.ds(first, count)
                s = lax.dot_general(q_ref[0, at, cols], k_ref[seen, cols], NT, preferred_element_type=jnp.float32)
                if kind != 1:
                    qi = part * tile + lax.broadcasted_iota(jnp.int32, (tile, count), 0)
                    ki = first + lax.broadcasted_iota(jnp.int32, (tile, count), 1)
                    s = jnp.where(ki <= qi if kind == 0 else ki > qi, s, LOW)
                top = jnp.max(s, axis=1, keepdims=True) * scale
                p = jnp.exp2(s * scale - top)
                if kind == 2:
                    p = jnp.where(ki > qi, p, 0.0)
                v = jnp.concatenate([v_ref[seen, cols], jnp.ones((count, size), jnp.bfloat16)], axis=1)
                both = jnp.dot(p.astype(jnp.bfloat16), v, preferred_element_type=jnp.float32)
                acc[at, cols] = both[:, :size]
                lref[at, cols] = both[:, size:]
                mref[at, cols] = jnp.broadcast_to(jnp.maximum(top, LOW), (tile, size))

    @pl.when(dist == 0)
    def _():
        near(0)

    @pl.when((dist > 0) & (dist < SPAN))
    def _():
        near(1)

    @pl.when(dist == SPAN)
    def _():
        near(2)

    @pl.when((dist < 0) | (dist > SPAN))
    def _():
        acc[...] = jnp.zeros_like(acc)
        lref[...] = jnp.zeros_like(lref)
        mref[...] = jnp.full_like(mref, LOW)

    number = table_ref[src, capacity]

    def slots(i, carry):
        work = []
        for j in range(2):
            at_slot = 2 * i + j
            packed = table_ref[src, at_slot]
            at = pl.ds(pl.multiple_of((packed // blocks_held) * QBLK, QBLK), QBLK)
            mat = pl.ds(pl.multiple_of((packed % blocks_held) * QBLK, QBLK), QBLK)
            for h in range(heads):
                work.append((at, mat, slice(h * size, (h + 1) * size), h, at_slot < number))
        raw = [
            lax.dot_general(q_ref[0, at, cols], mk_ref[mat, cols], NT, preferred_element_type=jnp.float32)
            for at, mat, cols, h, real in work
        ]
        raw = [
            jnp.where(real, s * scale + gate_ref[h] * LOG2E, 2 * LOW)
            for s, (at, mat, cols, h, real) in zip(raw, work)
        ]
        tops = [jnp.max(s, axis=1, keepdims=True) for s in raw]
        probs = [jnp.exp2(s - top).astype(jnp.bfloat16) for s, top in zip(raw, tops)]
        ones = jnp.ones((QBLK, size), jnp.bfloat16)
        sums = [
            jnp.dot(p, jnp.concatenate([mv_ref[mat, cols], ones], axis=1), preferred_element_type=jnp.float32)
            for p, (at, mat, cols, h, real) in zip(probs, work)
        ]
        for top, both, (at, mat, cols, h, real) in zip(tops, sums, work):
            old = mref[at, cols]
            new = jnp.maximum(old, top)
            keep = jnp.exp2(old - new)
            add = jnp.exp2(top - new)
            acc[at, cols] = acc[at, cols] * keep + both[:, :size] * add
            lref[at, cols] = lref[at, cols] * keep + both[:, size:] * add
            mref[at, cols] = new
        return carry

    lax.fori_loop(0, (number + 1) // 2, slots, 0)

    step = 128

    @pl.loop(0, rows // step)
    def _(r):
        at = pl.ds(pl.multiple_of(r * step, step), step)
        lane = lax.broadcasted_iota(jnp.int32, (step, 128), 1)
        tops = jnp.full((step, 128), LOW, jnp.float32)
        sums = jnp.ones((step, 128), jnp.float32)
        for h in range(heads):
            cols = slice(h * size, (h + 1) * size)
            l = lref[at, cols]
            safe = jnp.where(l > 0.0, l, 1.0)
            o_ref[0, at, cols] = (acc[at, cols] / safe).astype(jnp.bfloat16)
            tops = jnp.where(lane == h, mref[at, cols], tops)
            sums = jnp.where(lane == h, safe, sums)
        lse_ref[0, :, at] = (tops + jnp.log2(sums)).T[: lse_ref.shape[1]]


def partials(q_all, keys, values, mkeys, mvalues, gate, place, table, capacity, group):
    sources, rows, width = q_all.shape
    heads = gate.shape[0]
    stat_rows = -(-heads // 8) * 8
    side = lambda a: pl.BlockSpec((a.shape[0], width), lambda s: (0, group))
    smem = pl.BlockSpec(memory_space=pltpu.SMEM)
    per = pl.BlockSpec((1, rows, width), lambda s: (s, 0, 0))
    return pl.pallas_call(
        functools.partial(local_kernel, heads, mkeys.shape[0] // QBLK, capacity),
        grid=(sources,),
        in_specs=[smem, smem, smem, per, side(keys), side(values), side(mkeys), side(mvalues)],
        out_specs=[per, pl.BlockSpec((1, stat_rows, rows), lambda s: (s, 0, 0))],
        out_shape=[
            jax.ShapeDtypeStruct(q_all.shape, jnp.bfloat16),
            jax.ShapeDtypeStruct((sources, stat_rows, rows), jnp.float32),
        ],
        scratch_shapes=[pltpu.VMEM((rows, width), jnp.float32)] * 3,
        compiler_params=pltpu.CompilerParams(vmem_limit_bytes=56 * 2**20),
        cost_estimate=pl.CostEstimate(
            flops=20 * rows * rows * width, bytes_accessed=64 * rows * width, transcendentals=rows * rows * heads
        ),
    )(place, table, gate, q_all, keys, values, mkeys, mvalues)


def merge_kernel(
    heads, chips, halves, o_a, lse_a, o_b, lse_b, out_ref,
    own, own_s, twin, twin_s, left, left_s, right, right_s,
    load_sem, load_s_sem, tsend, tsend_s, trecv, trecv_s,
    usend, usend_s, urecv, urecv_s, dsend, dsend_s, drecv, drecv_s,
):
    c = lax.axis_index("ctx")
    m = lax.axis_index("mem")
    rows, width = out_ref.shape
    size = width // heads
    half = rows // halves
    wide = width // 2
    last = chips - 1
    hbm = ((o_a, lse_a), (o_b, lse_b))

    barrier = pltpu.get_barrier_semaphore()
    pl.semaphore_signal(barrier, inc=1, device_id={"mem": 1 - m}, device_id_type=MESH)

    @pl.when(c > 0)
    def _():
        pl.semaphore_signal(barrier, inc=1, device_id={"ctx": c - 1}, device_id_type=MESH)

    @pl.when(c < last)
    def _():
        pl.semaphore_signal(barrier, inc=1, device_id={"ctx": c + 1}, device_id_type=MESH)

    inner = (c > 0).astype(jnp.int32) + (c < last).astype(jnp.int32)
    pl.semaphore_wait(barrier, 1 + inner)

    def remote(src, dst, ss, rs, where):
        return pltpu.make_async_remote_copy(
            src_ref=src, dst_ref=dst, send_sem=ss, recv_sem=rs, device_id=where, device_id_type=MESH
        )

    def spots(g, d, r):
        at = pl.ds(pl.multiple_of(r * half, half), half)
        return (g, d, at), (g, d, slice(None), at), (at, (slice(None), at)), (g * chips + d) * halves + r

    def loads(g, d, r):
        big, small, (at, at_s), n = spots(g, d, r)
        o_hbm, lse_hbm = hbm[g]
        return (
            pltpu.make_async_copy(o_hbm.at[2 * d + m, at], own.at[big], load_sem.at[n]),
            pltpu.make_async_copy(lse_hbm.at[2 * d + m, :, at], own_s.at[small], load_s_sem.at[n]),
        )

    def twins(g, d, r):
        big, small, (at, at_s), n = spots(g, d, r)
        o_hbm, lse_hbm = hbm[g]
        other = {"mem": 1 - m}
        return (
            remote(o_hbm.at[2 * d + 1 - m, at], twin.at[big], tsend.at[n], trecv.at[n], other),
            remote(lse_hbm.at[2 * d + 1 - m, :, at], twin_s.at[small], tsend_s.at[n], trecv_s.at[n], other),
        )

    def ups(g, d, r):
        big, small, _, n = spots(g, d, r)
        where = {"ctx": c + 1}
        return (
            remote(own.at[big], left.at[big], usend.at[n], urecv.at[n], where),
            remote(own_s.at[small], left_s.at[small], usend_s.at[n], urecv_s.at[n], where),
        )

    def downs(g, d, r):
        big, small, _, n = spots(g, d, r)
        where = {"ctx": c - 1}
        return (
            remote(own.at[big], right.at[big], dsend.at[n], drecv.at[n], where),
            remote(own_s.at[small], right_s.at[small], dsend_s.at[n], drecv_s.at[n], where),
        )

    order = []
    for i in range(chips):
        for d in (last - i, i):
            if d not in order:
                order.append(d)
    for d in order:
        for g in range(2):
            @pl.loop(0, halves)
            def _(r):
                for copy in twins(g, d, r) + loads(g, d, r):
                    copy.start()

    def combine(g, d, r, into, others):
        big, small, _, _ = spots(g, d, r)
        parts = [own] + [o for o, _ in others]
        stats = [own_s[small]] + [s[small] for _, s in others]
        top = functools.reduce(jnp.maximum, stats)
        weights = [jnp.exp2(s - top) for s in stats]
        total = functools.reduce(jnp.add, weights)
        own_s[small] = top + jnp.log2(total)
        shares = [(w / total).T for w in weights]
        step = 64
        for t in range(half // step):
            at = pl.ds(pl.multiple_of(r * half + t * step, step), step)
            for h in range(heads // 2):
                cols = slice(h * size, (h + 1) * size)
                out = None
                for part, share in zip(parts, shares):
                    term = part[g, d, at, cols].astype(jnp.float32) * share[t * step : (t + 1) * step, h : h + 1]
                    out = term if out is None else out + term
                into(at, cols, out.astype(jnp.bfloat16))

    def wait_local(g, d, r):
        for copy in loads(g, d, r):
            copy.wait()
        for copy in twins(g, d, r):
            copy.wait()

    def store_own(g, d):
        def put(at, cols, value):
            own[g, d, at, cols] = value
        return put

    def store_out(g):
        def put(at, cols, value):
            out_ref[at, g * wide + cols.start : g * wide + cols.stop] = value
        return put

    def visit(g, d, r, copies, first, arrived):
        wait_local(g, d, r)

        @pl.when(first)
        def _():
            combine(g, d, r, store_own(g, d), [(twin, twin_s)])

        @pl.when(jnp.logical_not(first))
        def _():
            for copy in copies(g, d, r):
                copy.wait_recv()
            combine(g, d, r, store_own(g, d), [(twin, twin_s), arrived])

        for copy in copies(g, d, r):
            copy.start()

    @pl.loop(0, last)
    def _(i):
        for g in range(2):
            @pl.loop(0, halves)
            def _(r):
                @pl.when(last - i > c)
                def _():
                    visit(g, last - i, r, ups, c == 0, (left, left_s))

                @pl.when(i < c)
                def _():
                    visit(g, i, r, downs, c == last, (right, right_s))

    for g in range(2):
        @pl.loop(0, halves)
        def _(r):
            wait_local(g, c, r)

            @pl.when(c == 0)
            def _():
                for copy in downs(g, c, r):
                    copy.wait_recv()
                combine(g, c, r, store_out(g), [(twin, twin_s), (right, right_s)])

            @pl.when(c == last)
            def _():
                for copy in ups(g, c, r):
                    copy.wait_recv()
                combine(g, c, r, store_out(g), [(twin, twin_s), (left, left_s)])

            @pl.when((c > 0) & (c < last))
            def _():
                for copy in ups(g, c, r) + downs(g, c, r):
                    copy.wait_recv()
                combine(g, c, r, store_out(g), [(twin, twin_s), (left, left_s), (right, right_s)])

    @pl.loop(0, chips)
    def _(d):
        for g in range(2):
            @pl.loop(0, halves)
            def _(r):
                @pl.when(d > c)
                def _():
                    for copy in ups(g, d, r):
                        copy.wait_send()

                @pl.when(d < c)
                def _():
                    for copy in downs(g, d, r):
                        copy.wait_send()


def merged(first, second, heads):
    (o_a, lse_a), (o_b, lse_b) = first, second
    sources, rows, width = o_a.shape
    chips = sources // 2
    halves = 2 if chips <= 4 else 1
    big = pltpu.VMEM((2, chips, rows, width), jnp.bfloat16)
    small = pltpu.VMEM((2, chips) + lse_a.shape[1:], jnp.float32)
    return pl.pallas_call(
        functools.partial(merge_kernel, heads, chips, halves),
        in_specs=[pl.BlockSpec(memory_space=pl.ANY)] * 4,
        out_specs=pl.BlockSpec(memory_space=pltpu.VMEM),
        out_shape=jax.ShapeDtypeStruct((rows, 2 * width), jnp.bfloat16),
        scratch_shapes=[big, small] * 4 + [pltpu.SemaphoreType.DMA((2 * chips * halves,))] * 14,
        compiler_params=pltpu.CompilerParams(
            collective_id=0, has_side_effects=True, vmem_limit_bytes=56 * 2**20
        ),
    )(o_a, lse_a, o_b, lse_b)


def body(queries, keys, values, memory_keys, memory_values, retrieval, memory_gate):
    axes = ("ctx", "mem")
    sources = lax.axis_size(axes)
    place = lax.axis_index(axes)
    query_blocks, topk = retrieval.shape
    capacity = max(3, 3 * query_blocks * topk // (2 * sources))
    blocks_held = memory_keys.shape[0] // QBLK
    heads = memory_gate.shape[0]
    wide = queries.shape[1] // 2
    everyone = lax.all_gather(retrieval, axes, axis=0, tiled=True)
    table = slot_tables(everyone, place, blocks_held, sources, capacity)
    q_a = lax.all_gather(queries[:, :wide], axes, axis=0)
    later, q_a, table = lax.optimization_barrier((queries[:, wide:], q_a, table))
    q_b = lax.all_gather(later, axes, axis=0)
    where = place.reshape(1).astype(jnp.int32)
    sides = (keys, values, memory_keys, memory_values)
    first = partials(q_a, *sides, memory_gate[: heads // 2], where, table, capacity, 0)
    second = partials(q_b, *sides, memory_gate[heads // 2 :], where, table, capacity, 1)
    return merged(first, second, heads)


def solution(mesh):
    rows = P(("groups", "ctx", "mem"), "head")
    return jax.shard_map(
        body,
        mesh=mesh,
        in_specs=(rows, rows, rows, rows, rows, P(("groups", "ctx", "mem"), None), P("head")),
        out_specs=rows,
        check_vma=False,
    )
```

time: 424 us -> 244 us (0.58)
  the two profiles are of different devices: /device:TPU:20 before, /device:TPU:16 now
where the time goes in v2:
time: 244 us
  Pallas kernels  164 us (67%)
  waiting for transfers between devices  46.2 us (19%)
  between operations  13.4 us (5%)
  blocking collectives  12.3 us (5%)
  local copies, waits for them, and re-layouts  6.22 us (3%)
    pallas_call x1, Pallas kernels, merged(): pl.pallas_call(functools.partial(merge_kernel, heads, chips, halves), in_...  98.3 us
    pallas_call x2, Pallas kernels, partials(): pl.pallas_call(functools.partial(local_kernel, heads, mkeys.shape[0] // Q...  65.6 us
    all_gather x1, waiting for transfers between devices, body(): q_a = lax.all_gather(queries[:, :wide], axes, axis=0)  32.8 us
    all_gather x1, waiting for transfers between devices, body(): q_b = lax.all_gather(later, axes, axis=0)  13.3 us
    all_gather x1, blocking collectives, body(): everyone = lax.all_gather(retrieval, axes, axis=0, tiled=True)  12.3 us
  transfers between devices with their start and end apart: 2, of which 2 were waited for; matrix products, arithmetic and copies ran while one was open for 1% of the time, Pallas kernels for 13%

profile of v2, /device:TPU:16, one launch (start us, length us, event | category | flops | bytes accessed | tf_op | source)
XLA Modules:
  0.0 243.6 jit_solution(382529402013623054)
XLA Ops:
  6.5 0.0 all-gather.5.cloned.1.call-start
  6.5 2.3 fusion.11
  8.8 0.0 all-gather.5.cloned.1.call-update
  8.8 0.0 all-gather.7.cloned.1.call-start
  8.9 12.3 %all_gather.17 = s32[64,8]{1,0:T(8,128)S(1)} all-gather(s32[8,8]{1,0:T(8,128)} %param.12), channel_id=1, replica_groups=mesh['groups'=2,'ctx'=4,'head'=2,'mem'=2] {'ctx','mem'}, dimensions={0}, use_global_device_ids=true | all-gather | bytes 2304 | tf_op jit(solution)/shard_map/all_gather | solution.py:385
  21.2 0.1 reshape.149
  21.3 0.1 convert_reduce_fusion
  21.4 0.1 reduce_sum.27
  21.5 0.1 reduce_sum.28
  21.6 0.1 copy.11
  21.7 0.2 reduce_window_sum.11
  22.0 0.3 select_reduce_fusion
  22.3 0.1 copy.10
  22.3 0.7 pad_add_fusion.table_ref
  23.0 32.8 %all-gather.5.cloned.1.call-done = bf16[4096,512]{1,0:T(8,128)(2,1)} async-done(((bf16[512,512]{1,0:T(8,128)(2,1)}), bf16[4096,512]{1,0:T(8,128)(2,1)}) %all-gather.5.cloned.1.call-update) | async-done | bytes 4194320 | tf_op jit(solution)/shard_map/all_gather | solution.py:387
  55.8 0.0 all-gather.7.cloned.1.call-update
  55.9 1.4 fusion.12
  57.2 32.8 %shard_map.73 = (bf16[8,512,512]{2,1,0:T(8,128)(2,1)}, f32[8,8,512]{2,1,0:T(8,128)}) custom-call(s32[1]{0:T(128)} %bitcast.place_ref, s32[8,13]{1,0:T(8,128)} %pad_add_fusion.table_ref, f32[4]{0:T(128)} %get-tuple-element.24.gate_ref, bf16[8,512,512]{2,1,0:T(8,128)(2,1)} %bitcast.4, bf16[512,1024]{1,0:T(8,128)(2,1)} %k_ref.3, bf16[512,1024]{1,0:T(8,128)(2,1)} %v_ref.3, ...), custom_call_target="tpu_custom_call" | custom-call | flops 2684354560 | bytes 16777216 | tf_op jit(solution)/shard_map/pallas_call | solution.py:153
  90.1 13.3 %all-gather.7.cloned.1.call-done = bf16[4096,512]{1,0:T(8,128)(2,1)} async-done(((bf16[512,512]{1,0:T(8,128)(2,1)}), bf16[4096,512]{1,0:T(8,128)(2,1)}) %all-gather.7.cloned.1.call-update) | async-done | bytes 4194320 | tf_op jit(solution)/shard_map/all_gather | solution.py:389
  103.4 32.8 %shard_map.74 = (bf16[8,512,512]{2,1,0:T(8,128)(2,1)}, f32[8,8,512]{2,1,0:T(8,128)}) custom-call(s32[1]{0:T(128)} %bitcast.place_ref, s32[8,13]{1,0:T(8,128)} %pad_add_fusion.table_ref, f32[4]{0:T(128)} %get-tuple-element.23.gate_ref, bf16[8,512,512]{2,1,0:T(8,128)(2,1)} %bitcast.5, bf16[512,1024]{1,0:T(8,128)(2,1)} %k_ref.3, bf16[512,1024]{1,0:T(8,128)(2,1)} %v_ref.3, ...), custom_call_target="tpu_custom_call" | custom-call | flops 2684354560 | bytes 16777216 | tf_op jit(solution)/shard_map/pallas_call | solution.py:153
  136.2 98.3 %shard_map.75 = bf16[512,1024]{1,0:T(8,128)(2,1)} custom-call(bf16[8,512,512]{2,1,0:T(8,128)(2,1)} %get-tuple-element.14.o_a, f32[8,8,512]{2,1,0:T(8,128)} %get-tuple-element.15.lse_a, bf16[8,512,512]{2,1,0:T(8,128)(2,1)} %get-tuple-element.17.o_b, f32[8,8,512]{2,1,0:T(8,128)} %get-tuple-element.18.lse_b), custom_call_target="tpu_custom_call" | custom-call | tf_op jit(solution)/shard_map/pallas_call | solution.py:364
  234.5 2.3 copy.13
  (3 shorter events, 0.0 us)
Async XLA Ops:
  6.5 49.3 %all-gather.5.cloned.1.call-start = ((), (), s32[]{:S(2)}) async-start(), calls=%async_computation | async-start | bytes 4718592 | tf_op jit(solution)/shard_map/all_gather | solution.py:387
  8.8 94.6 %all-gather.7.cloned.1.call-start = ((), (), s32[]{:S(2)}) async-start(), calls=%async_computation.1 | async-start | bytes 4718592 | tf_op jit(solution)/shard_map/all_gather | solution.py:389
Sparse Core Ops, SparseCore 0:
  9.0 46.8 all-gather.4
  57.4 45.9 all-gather.6

commit v3 on v2

--- a/solution.py
+++ b/solution.py
@@ -144,7 +144,8 @@
 
 
 def partials(q_all, keys, values, mkeys, mvalues, gate, place, table, capacity, group):
-    sources, rows, width = q_all.shape
+    sources, _, width = q_all.shape
+    rows = keys.shape[0]
     heads = gate.shape[0]
     stat_rows = -(-heads // 8) * 8
     side = lambda a: pl.BlockSpec((a.shape[0], width), lambda s: (0, group))
@@ -156,7 +157,7 @@
         in_specs=[smem, smem, smem, per, side(keys), side(values), side(mkeys), side(mvalues)],
         out_specs=[per, pl.BlockSpec((1, stat_rows, rows), lambda s: (s, 0, 0))],
         out_shape=[
-            jax.ShapeDtypeStruct(q_all.shape, jnp.bfloat16),
+            jax.ShapeDtypeStruct((sources, rows, width), jnp.bfloat16),
             jax.ShapeDtypeStruct((sources, stat_rows, rows), jnp.float32),
         ],
         scratch_shapes=[pltpu.VMEM((rows, width), jnp.float32)] * 3,
@@ -373,6 +374,105 @@
     )(o_a, lse_a, o_b, lse_b)
 
 
+def gather_kernel(chips, q_ref, out_ref, own_sem, usend, urecv, dsend, drecv, tsend, trecv):
+    c = lax.axis_index("ctx")
+    m = lax.axis_index("mem")
+    last = chips - 1
+    barrier = pltpu.get_barrier_semaphore()
+    pl.semaphore_signal(barrier, inc=1, device_id={"mem": 1 - m}, device_id_type=MESH)
+
+    @pl.when(c > 0)
+    def _():
+        pl.semaphore_signal(barrier, inc=1, device_id={"ctx": c - 1}, device_id_type=MESH)
+
+    @pl.when(c < last)
+    def _():
+        pl.semaphore_signal(barrier, inc=1, device_id={"ctx": c + 1}, device_id_type=MESH)
+
+    inner = (c > 0).astype(jnp.int32) + (c < last).astype(jnp.int32)
+    pl.semaphore_wait(barrier, 1 + inner)
+
+    def copy(src, d, sends, recvs, where):
+        return pltpu.make_async_remote_copy(
+            src_ref=src, dst_ref=out_ref.at[2 * d + m], send_sem=sends.at[d], recv_sem=recvs.at[d],
+            device_id=where, device_id_type=MESH,
+        )
+
+    def up(src, d):
+        return copy(src, d, usend, urecv, {"ctx": c + 1})
+
+    def down(src, d):
+        return copy(src, d, dsend, drecv, {"ctx": c - 1})
+
+    def twin(src, d):
+        return copy(src, d, tsend, trecv, {"mem": 1 - m})
+
+    @pl.when(c < last)
+    def _():
+        up(q_ref, c).start()
+
+    @pl.when(c > 0)
+    def _():
+        down(q_ref, c).start()
+
+    twin(q_ref, c).start()
+    own = pltpu.make_async_copy(q_ref, out_ref.at[2 * c + m], own_sem)
+    own.start()
+
+    @pl.loop(0, last)
+    def _(t):
+        low = c - 1 - t
+        high = c + 1 + t
+
+        @pl.when(low >= 0)
+        def _():
+            block = out_ref.at[2 * low + m]
+            up(block, low).wait_recv()
+
+            @pl.when(c < last)
+            def _():
+                up(block, low).start()
+
+            twin(block, low).start()
+
+        @pl.when(high <= last)
+        def _():
+            block = out_ref.at[2 * high + m]
+            down(block, high).wait_recv()
+
+            @pl.when(c > 0)
+            def _():
+                down(block, high).start()
+
+            twin(block, high).start()
+
+    own.wait()
+
+    @pl.loop(0, chips)
+    def _(d):
+        twin(q_ref, d).wait()
+
+        @pl.when((d <= c) & (c < last))
+        def _():
+            up(q_ref, d).wait_send()
+
+        @pl.when((d >= c) & (c > 0))
+        def _():
+            down(q_ref, d).wait_send()
+
+
+def gathered(q, sources):
+    chips = sources // 2
+    return pl.pallas_call(
+        functools.partial(gather_kernel, chips),
+        in_specs=[pl.BlockSpec(memory_space=pl.ANY)],
+        out_specs=pl.BlockSpec(memory_space=pl.ANY),
+        out_shape=jax.ShapeDtypeStruct((sources,) + q.shape, q.dtype),
+        scratch_shapes=[pltpu.SemaphoreType.DMA] + [pltpu.SemaphoreType.DMA((chips,))] * 6,
+        compiler_params=pltpu.CompilerParams(collective_id=1, has_side_effects=True),
+    )(q)
+
+
 def body(queries, keys, values, memory_keys, memory_values, retrieval, memory_gate):
     axes = ("ctx", "mem")
     sources = lax.axis_size(axes)
@@ -382,11 +482,16 @@
     blocks_held = memory_keys.shape[0] // QBLK
     heads = memory_gate.shape[0]
     wide = queries.shape[1] // 2
-    everyone = lax.all_gather(retrieval, axes, axis=0, tiled=True)
+    tok_rows = queries.shape[0]
+    ids = retrieval.reshape(1, -1)
+    halves = jnp.concatenate([ids // 256, ids % 256], axis=0).astype(queries.dtype)
+    tail = jnp.pad(halves, ((0, 14), (0, wide - ids.shape[1])))
+    q_a = gathered(jnp.concatenate([queries[:, :wide], tail], axis=0), sources)
+    later, q_a = lax.optimization_barrier((queries[:, wide:], q_a))
+    q_b = lax.all_gather(later, axes, axis=0)
+    got = q_a[:, tok_rows : tok_rows + 2, : ids.shape[1]].astype(jnp.int32)
+    everyone = (got[:, 0] * 256 + got[:, 1]).reshape(-1, topk)
     table = slot_tables(everyone, place, blocks_held, sources, capacity)
-    q_a = lax.all_gather(queries[:, :wide], axes, axis=0)
-    later, q_a, table = lax.optimization_barrier((queries[:, wide:], q_a, table))
-    q_b = lax.all_gather(later, axes, axis=0)
     where = place.reshape(1).astype(jnp.int32)
     sides = (keys, values, memory_keys, memory_values)
     first = partials(q_a, *sides, memory_gate[: heads // 2], where, table, capacity, 0)

time: 244 us -> 238 us (0.975)
  Pallas kernels: 164 us -> 199 us
  waiting for transfers between devices: 46.2 us -> 17.8 us
  blocking collectives: 12.3 us -> 0 us
    pallas_call x0 -> x1, Pallas kernels: none -> 37.4 us  [gathered(): pl.pallas_call(functools.partial(gather_kernel, chips), in_specs=[pl.Bloc...]
    all_gather x1 -> x0, waiting for transfers between devices: 32.8 us -> none  [body(): q_a = lax.all_gather(queries[:, :wide], axes, axis=0)]
    all_gather x1 -> x0, blocking collectives: 12.3 us -> none  [body(): everyone = lax.all_gather(retrieval, axes, axis=0, tiled=True)]
    pallas_call x2, Pallas kernels: 65.6 us -> 61.1 us  [partials(): pl.pallas_call(functools.partial(local_kernel, heads, mkeys.shape[0] // Q...]
    all_gather x1, waiting for transfers between devices: 13.3 us -> 17.8 us  [body(): q_b = lax.all_gather(later, axes, axis=0)]
  transfers between devices with their start and end apart: 2 -> 1, of which waited for: 2 -> 1; matrix products, arithmetic and copies ran while one was open for 1% -> 1% of each run, Pallas kernels for 13% -> 13%
where the time goes in v3:
time: 238 us; the launch traced here: 239 us
  Pallas kernels  199 us (84%)
  waiting for transfers between devices  17.8 us (7%)
  between operations  13.4 us (6%)
  local copies, waits for them, and re-layouts  5.87 us (2%)
  other arithmetic  2.91 us (1%)
    pallas_call x1, Pallas kernels, merged(): pl.pallas_call(functools.partial(merge_kernel, heads, chips, halves), in_...  100 us
    pallas_call x2, Pallas kernels, partials(): pl.pallas_call(functools.partial(local_kernel, heads, mkeys.shape[0] // Q...  61.1 us
    pallas_call x1, Pallas kernels, gathered(): pl.pallas_call(functools.partial(gather_kernel, chips), in_specs=[pl.Bloc...  37.4 us
    all_gather x1, waiting for transfers between devices, body(): q_b = lax.all_gather(later, axes, axis=0)  17.8 us
  transfers between devices with their start and end apart: 1, of which 1 were waited for; matrix products, arithmetic and copies ran while one was open for 1% of the time, Pallas kernels for 13%

profile of v3, /device:TPU:16, one launch (start us, length us, event | category | flops | bytes accessed | tf_op | source)
XLA Modules:
  0.0 238.6 jit_solution(14645649966619771698)
XLA Ops:
  6.5 0.0 copy-start
  6.5 0.0 all-gather.3.cloned.1.call-start
  6.5 2.1 fusion.16
  8.6 0.8 reshape.281
  9.4 0.8 pad_maximum_fusion.q_ref
  10.3 37.4 %shard_map.73.q_ref = bf16[8,528,512]{2,1,0:T(8,128)(2,1)} custom-call(bf16[528,512]{1,0:T(8,128)(2,1)} %pad_maximum_fusion.q_ref), custom_call_target="tpu_custom_call" | custom-call | tf_op jit(solution)/shard_map/pallas_call | solution.py:466
  47.7 0.0 all-gather.3.cloned.1.call-update
  47.7 0.7 slice_convert_fusion
  48.5 0.1 convert_reduce_fusion
  48.6 0.1 copy.10
  48.7 0.2 reduce_window_sum.11
  48.9 0.3 select_reduce_fusion
  49.2 0.1 copy.9
  49.3 0.7 pad_add_fusion.table_ref
  49.9 0.0 copy-done
  49.9 0.6 fusion.17
  50.5 30.5 %shard_map.74 = (bf16[8,512,512]{2,1,0:T(8,128)(2,1)}, f32[8,8,512]{2,1,0:T(8,128)}) custom-call(s32[1]{0:T(128)} %bitcast.place_ref, s32[8,13]{1,0:T(8,128)} %pad_add_fusion.table_ref, f32[4]{0:T(128)} %get-tuple-element.22.gate_ref, bf16[8,528,512]{2,1,0:T(8,128)(2,1)} %shard_map.73.q_ref, bf16[512,1024]{1,0:T(8,128)(2,1)} %k_ref.3, ...), custom_call_target="tpu_custom_call" | custom-call | flops 2684354560 | bytes 16777216 | tf_op jit(solution)/shard_map/pallas_call | solution.py:154
  81.1 17.8 %all-gather.3.cloned.1.call-done = bf16[4096,512]{1,0:T(8,128)(2,1)} async-done(((bf16[512,512]{1,0:T(8,128)(2,1)}), bf16[4096,512]{1,0:T(8,128)(2,1)}) %all-gather.3.cloned.1.call-update) | async-done | bytes 4194320 | tf_op jit(solution)/shard_map/all_gather | solution.py:491
  98.9 30.5 %shard_map.75 = (bf16[8,512,512]{2,1,0:T(8,128)(2,1)}, f32[8,8,512]{2,1,0:T(8,128)}) custom-call(s32[1]{0:T(128)} %bitcast.place_ref, s32[8,13]{1,0:T(8,128)} %pad_add_fusion.table_ref, f32[4]{0:T(128)} %get-tuple-element.21.gate_ref, bf16[8,512,512]{2,1,0:T(8,128)(2,1)} %bitcast.4, bf16[512,1024]{1,0:T(8,128)(2,1)} %k_ref.3, bf16[512,1024]{1,0:T(8,128)(2,1)} %v_ref.3, ...), custom_call_target="tpu_custom_call" | custom-call | flops 2684354560 | bytes 16777216 | tf_op jit(solution)/shard_map/pallas_call | solution.py:154
  129.4 100.1 %shard_map.76 = bf16[512,1024]{1,0:T(8,128)(2,1)} custom-call(bf16[8,512,512]{2,1,0:T(8,128)(2,1)} %get-tuple-element.12.o_a, f32[8,8,512]{2,1,0:T(8,128)} %get-tuple-element.13.lse_a, bf16[8,512,512]{2,1,0:T(8,128)(2,1)} %get-tuple-element.15.o_b, f32[8,8,512]{2,1,0:T(8,128)} %get-tuple-element.16.lse_b), custom_call_target="tpu_custom_call" | custom-call | tf_op jit(solution)/shard_map/pallas_call | solution.py:365
  229.5 2.3 copy.12
  (6 shorter events, 0.1 us)
Async XLA Ops:
  6.5 43.4 %copy-start = (f32[8]{0:T(128)S(1)}, f32[8]{0:T(128)}, u32[]{:S(2)}) copy-start(f32[8]{0:T(128)} %param.13) | copy-start | bytes 100
  6.5 92.3 %all-gather.3.cloned.1.call-start = ((), (), s32[]{:S(2)}) async-start(), calls=%async_computation | async-start | bytes 4718592 | tf_op jit(solution)/shard_map/all_gather | solution.py:491
Sparse Core Ops, SparseCore 0:
  47.8 51.0 all-gather.2

commit v4 on v3

--- a/solution.py
+++ b/solution.py
@@ -359,7 +359,7 @@
     (o_a, lse_a), (o_b, lse_b) = first, second
     sources, rows, width = o_a.shape
     chips = sources // 2
-    halves = 2 if chips <= 4 else 1
+    halves = 4 if chips <= 4 else 1
     big = pltpu.VMEM((2, chips, rows, width), jnp.bfloat16)
     small = pltpu.VMEM((2, chips) + lse_a.shape[1:], jnp.float32)
     return pl.pallas_call(

time: 238 us -> 258 us (1.084); the launches traced: 239 us -> 256 us
  Pallas kernels: 199 us -> 217 us
    pallas_call x1, Pallas kernels: 100 us -> 116 us  [merged(): pl.pallas_call(functools.partial(merge_kernel, heads, chips, halves), in_...]
    pallas_call x2, Pallas kernels: 61.1 us -> 63.8 us  [partials(): pl.pallas_call(functools.partial(local_kernel, heads, mkeys.shape[0] // Q...]
  transfers between devices with their start and end apart: 1 -> 1, of which waited for: 1 -> 1; matrix products, arithmetic and copies ran while one was open for 1% -> 1% of each run, Pallas kernels for 13% -> 12%
where the time goes in v4:
time: 258 us; the launch traced here: 256 us
  Pallas kernels  217 us (84%)
  waiting for transfers between devices  16.5 us (6%)
  between operations  13.4 us (5%)
  local copies, waits for them, and re-layouts  5.87 us (2%)
  other arithmetic  2.91 us (1%)
    pallas_call x1, Pallas kernels, merged(): pl.pallas_call(functools.partial(merge_kernel, heads, chips, halves), in_...  116 us
    pallas_call x2, Pallas kernels, partials(): pl.pallas_call(functools.partial(local_kernel, heads, mkeys.shape[0] // Q...  63.8 us
    pallas_call x1, Pallas kernels, gathered(): pl.pallas_call(functools.partial(gather_kernel, chips), in_specs=[pl.Bloc...  37.4 us
    all_gather x1, waiting for transfers between devices, body(): q_b = lax.all_gather(later, axes, axis=0)  16.4 us
  transfers between devices with their start and end apart: 1, of which 1 were waited for; matrix products, arithmetic and copies ran while one was open for 1% of the time, Pallas kernels for 12%

profile of v4, /device:TPU:16, one launch (start us, length us, event | category | flops | bytes accessed | tf_op | source)
XLA Modules:
  0.0 255.9 jit_solution(15616416054087170380)
XLA Ops:
  6.5 0.0 copy-start
  6.5 0.0 all-gather.3.cloned.1.call-start
  6.5 2.1 fusion.16
  8.6 0.8 reshape.281
  9.4 0.8 pad_maximum_fusion.q_ref
  10.3 37.4 %shard_map.73.q_ref = bf16[8,528,512]{2,1,0:T(8,128)(2,1)} custom-call(bf16[528,512]{1,0:T(8,128)(2,1)} %pad_maximum_fusion.q_ref), custom_call_target="tpu_custom_call" | custom-call | tf_op jit(solution)/shard_map/pallas_call | solution.py:466
  47.7 0.0 all-gather.3.cloned.1.call-update
  47.7 0.7 slice_convert_fusion
  48.5 0.1 convert_reduce_fusion
  48.6 0.1 copy.10
  48.7 0.2 reduce_window_sum.11
  48.9 0.3 select_reduce_fusion
  49.2 0.1 copy.9
  49.3 0.7 pad_add_fusion.table_ref
  49.9 0.0 copy-done
  49.9 0.6 fusion.17
  50.5 31.9 %shard_map.74 = (bf16[8,512,512]{2,1,0:T(8,128)(2,1)}, f32[8,8,512]{2,1,0:T(8,128)}) custom-call(s32[1]{0:T(128)} %bitcast.place_ref, s32[8,13]{1,0:T(8,128)} %pad_add_fusion.table_ref, f32[4]{0:T(128)} %get-tuple-element.22.gate_ref, bf16[8,528,512]{2,1,0:T(8,128)(2,1)} %shard_map.73.q_ref, bf16[512,1024]{1,0:T(8,128)(2,1)} %k_ref.3, ...), custom_call_target="tpu_custom_call" | custom-call | flops 2684354560 | bytes 16777216 | tf_op jit(solution)/shard_map/pallas_call | solution.py:154
  82.4 16.4 %all-gather.3.cloned.1.call-done = bf16[4096,512]{1,0:T(8,128)(2,1)} async-done(((bf16[512,512]{1,0:T(8,128)(2,1)}), bf16[4096,512]{1,0:T(8,128)(2,1)}) %all-gather.3.cloned.1.call-update) | async-done | bytes 4194320 | tf_op jit(solution)/shard_map/all_gather | solution.py:491
  98.9 31.9 %shard_map.75 = (bf16[8,512,512]{2,1,0:T(8,128)(2,1)}, f32[8,8,512]{2,1,0:T(8,128)}) custom-call(s32[1]{0:T(128)} %bitcast.place_ref, s32[8,13]{1,0:T(8,128)} %pad_add_fusion.table_ref, f32[4]{0:T(128)} %get-tuple-element.21.gate_ref, bf16[8,512,512]{2,1,0:T(8,128)(2,1)} %bitcast.4, bf16[512,1024]{1,0:T(8,128)(2,1)} %k_ref.3, bf16[512,1024]{1,0:T(8,128)(2,1)} %v_ref.3, ...), custom_call_target="tpu_custom_call" | custom-call | flops 2684354560 | bytes 16777216 | tf_op jit(solution)/shard_map/pallas_call | solution.py:154
  130.8 116.0 %shard_map.76 = bf16[512,1024]{1,0:T(8,128)(2,1)} custom-call(bf16[8,512,512]{2,1,0:T(8,128)(2,1)} %get-tuple-element.12.o_a, f32[8,8,512]{2,1,0:T(8,128)} %get-tuple-element.13.lse_a, bf16[8,512,512]{2,1,0:T(8,128)(2,1)} %get-tuple-element.15.o_b, f32[8,8,512]{2,1,0:T(8,128)} %get-tuple-element.16.lse_b), custom_call_target="tpu_custom_call" | custom-call | tf_op jit(solution)/shard_map/pallas_call | solution.py:365
  246.8 2.3 copy.12
  (6 shorter events, 0.1 us)
Async XLA Ops:
  6.5 43.4 %copy-start = (f32[8]{0:T(128)S(1)}, f32[8]{0:T(128)}, u32[]{:S(2)}) copy-start(f32[8]{0:T(128)} %param.13) | copy-start | bytes 100
  6.5 92.3 %all-gather.3.cloned.1.call-start = ((), (), s32[]{:S(2)}) async-start(), calls=%async_computation | async-start | bytes 4718592 | tf_op jit(solution)/shard_map/all_gather | solution.py:491
Sparse Core Ops, SparseCore 0:
  47.8 51.0 all-gather.2

commit v5 on v4

--- a/solution.py
+++ b/solution.py
@@ -359,7 +359,7 @@
     (o_a, lse_a), (o_b, lse_b) = first, second
     sources, rows, width = o_a.shape
     chips = sources // 2
-    halves = 4 if chips <= 4 else 1
+    halves = 1
     big = pltpu.VMEM((2, chips, rows, width), jnp.bfloat16)
     small = pltpu.VMEM((2, chips) + lse_a.shape[1:], jnp.float32)
     return pl.pallas_call(

time: 258 us -> 247 us (0.957); the launches traced: 256 us -> 249 us
  Pallas kernels: 217 us -> 209 us
    pallas_call x1, Pallas kernels: 116 us -> 110 us  [merged(): pl.pallas_call(functools.partial(merge_kernel, heads, chips, halves), in_...]
where the time goes in v5:
time: 247 us; the launch traced here: 249 us
  Pallas kernels  209 us (85%)
  waiting for transfers between devices  17.4 us (7%)
  between operations  13.4 us (5%)
  local copies, waits for them, and re-layouts  5.87 us (2%)
  other arithmetic  2.91 us (1%)
    pallas_call x1, Pallas kernels, merged(): pl.pallas_call(functools.partial(merge_kernel, heads, chips, halves), in_...  110 us
    pallas_call x2, Pallas kernels, partials(): pl.pallas_call(functools.partial(local_kernel, heads, mkeys.shape[0] // Q...  62 us
    pallas_call x1, Pallas kernels, gathered(): pl.pallas_call(functools.partial(gather_kernel, chips), in_specs=[pl.Bloc...  37.4 us
    all_gather x1, waiting for transfers between devices, body(): q_b = lax.all_gather(later, axes, axis=0)  17.3 us
  transfers between devices with their start and end apart: 1, of which 1 were waited for; matrix products, arithmetic and copies ran while one was open for 1% of the time, Pallas kernels for 12%

profile of v5, /device:TPU:16, one launch (start us, length us, event | category | flops | bytes accessed | tf_op | source)
XLA Modules:
  0.0 248.5 jit_solution(1166644903826838247)
XLA Ops:
  6.5 0.0 copy-start
  6.5 0.0 all-gather.3.cloned.1.call-start
  6.5 2.1 fusion.16
  8.6 0.8 reshape.281
  9.4 0.8 pad_maximum_fusion.q_ref
  10.3 37.4 %shard_map.73.q_ref = bf16[8,528,512]{2,1,0:T(8,128)(2,1)} custom-call(bf16[528,512]{1,0:T(8,128)(2,1)} %pad_maximum_fusion.q_ref), custom_call_target="tpu_custom_call" | custom-call | tf_op jit(solution)/shard_map/pallas_call | solution.py:466
  47.7 0.0 all-gather.3.cloned.1.call-update
  47.7 0.7 slice_convert_fusion
  48.5 0.1 convert_reduce_fusion
  48.6 0.1 copy.10
  48.7 0.2 reduce_window_sum.11
  48.9 0.3 select_reduce_fusion
  49.2 0.1 copy.9
  49.3 0.7 pad_add_fusion.table_ref
  49.9 0.0 copy-done
  49.9 0.6 fusion.17
  50.5 31.0 %shard_map.74 = (bf16[8,512,512]{2,1,0:T(8,128)(2,1)}, f32[8,8,512]{2,1,0:T(8,128)}) custom-call(s32[1]{0:T(128)} %bitcast.place_ref, s32[8,13]{1,0:T(8,128)} %pad_add_fusion.table_ref, f32[4]{0:T(128)} %get-tuple-element.22.gate_ref, bf16[8,528,512]{2,1,0:T(8,128)(2,1)} %shard_map.73.q_ref, bf16[512,1024]{1,0:T(8,128)(2,1)} %k_ref.3, ...), custom_call_target="tpu_custom_call" | custom-call | flops 2684354560 | bytes 16777216 | tf_op jit(solution)/shard_map/pallas_call | solution.py:154
  81.5 17.3 %all-gather.3.cloned.1.call-done = bf16[4096,512]{1,0:T(8,128)(2,1)} async-done(((bf16[512,512]{1,0:T(8,128)(2,1)}), bf16[4096,512]{1,0:T(8,128)(2,1)}) %all-gather.3.cloned.1.call-update) | async-done | bytes 4194320 | tf_op jit(solution)/shard_map/all_gather | solution.py:491
  98.9 31.0 %shard_map.75 = (bf16[8,512,512]{2,1,0:T(8,128)(2,1)}, f32[8,8,512]{2,1,0:T(8,128)}) custom-call(s32[1]{0:T(128)} %bitcast.place_ref, s32[8,13]{1,0:T(8,128)} %pad_add_fusion.table_ref, f32[4]{0:T(128)} %get-tuple-element.21.gate_ref, bf16[8,512,512]{2,1,0:T(8,128)(2,1)} %bitcast.4, bf16[512,1024]{1,0:T(8,128)(2,1)} %k_ref.3, bf16[512,1024]{1,0:T(8,128)(2,1)} %v_ref.3, ...), custom_call_target="tpu_custom_call" | custom-call | flops 2684354560 | bytes 16777216 | tf_op jit(solution)/shard_map/pallas_call | solution.py:154
  129.9 109.5 %shard_map.76 = bf16[512,1024]{1,0:T(8,128)(2,1)} custom-call(bf16[8,512,512]{2,1,0:T(8,128)(2,1)} %get-tuple-element.12.o_a, f32[8,8,512]{2,1,0:T(8,128)} %get-tuple-element.13.lse_a, bf16[8,512,512]{2,1,0:T(8,128)(2,1)} %get-tuple-element.15.o_b, f32[8,8,512]{2,1,0:T(8,128)} %get-tuple-element.16.lse_b), custom_call_target="tpu_custom_call" | custom-call | tf_op jit(solution)/shard_map/pallas_call | solution.py:365
  239.4 2.3 copy.12
  (6 shorter events, 0.1 us)
Async XLA Ops:
  6.5 43.4 %copy-start = (f32[8]{0:T(128)S(1)}, f32[8]{0:T(128)}, u32[]{:S(2)}) copy-start(f32[8]{0:T(128)} %param.13) | copy-start | bytes 100
  6.5 92.3 %all-gather.3.cloned.1.call-start = ((), (), s32[]{:S(2)}) async-start(), calls=%async_computation | async-start | bytes 4718592 | tf_op jit(solution)/shard_map/all_gather | solution.py:491
Sparse Core Ops, SparseCore 0:
  47.8 51.0 all-gather.2
